TPU v7x, 256 devices: a whole 4x4x8 slice. The times are simulated.
256 devices in a mesh: seq: 32 (over x, y, core), ch: 8 (over z).
Axes of the slice: x: 4, y: 4, z: 8, core: 2. Of those that a mesh axis runs over, the one named last changes fastest.
Arguments:
- query_proj: bfloat16 [8192, 8192], P('seq', 'ch'), may hold values from -6 to 6
- key_projected: bfloat16 [8192, 8192], P('seq', 'ch'), may hold values from -6 to 6
- value_projected: bfloat16 [8192, 8192], P('seq', 'ch'), may hold values from -6 to 6
- mode_decay_speed: float32 [8192, 16], P('ch'), may hold values from 6.1035156e-05 to 0.04
- residue: float32 [8192, 16], P('ch'), may hold values from -1.5 to 1.5
- out_weight: bfloat16 [8192, 4096], P('ch'), may hold values from -0.09375 to 0.09375
Outputs:
- projected: bfloat16 [8192, 4096], P('seq', 'ch')
All inputs are finite; a program needn't handle non-finite values.
Results may differ from a plain program's by a relative error of at most 0.023.
Values may be sent and summed in bfloat16 or wider, within the bound.
A program may use at most 192 MiB of HBM per device.

v0:
```python
import functools

import jax
import jax.numpy as jnp
from jax import lax
from jax.experimental import pallas as pl
from jax.experimental.pallas import tpu as pltpu
from jax.sharding import PartitionSpec as P

MESH = pl.DeviceIdType.MESH
F32, BF16 = jnp.float32, jnp.bfloat16

ROWS = 256
WIDTH = 1024
COLS = 512
BLOCK = 64
CHIPS = 16

UNITS = [(0, 0), (1, 0), (2, 0), (3, 0), (0, 1), (1, 1), (2, 1), (3, 1), (0, 2), (1, 2), (2, 2), (3, 2), (0, 3), (1, 3)]
INDEX = {unit: at for at, unit in enumerate(UNITS)}


def distance(block, step):
    return (4 if block < 2 else 3) - step


def one_minus_exp(u):
    series = jnp.ones_like(u)
    for order in range(8, 1, -1):
        series = 1.0 - u * series * (1.0 / order)
    return jnp.where(u < 0.25, u * series, 1.0 - jnp.exp(-u))


def kernel(
    q_hbm, k_hbm, v_hbm, decay_hbm, residue_hbm, w_hbm, out_hbm,
    q_buf, k_buf, v_buf, decay_buf, residue_buf, w_buf,
    rate, ratio, weight, xs, ys, own, other, total, totals, carry, gated, part, sent, received, out_buf,
    load_sem, w_sem, core_send, core_recv, total_send, total_recv, carry_send, carry_recv, z_send, z_recv, out_sem,
):
    seq, z = lax.axis_index("seq"), lax.axis_index("ch")
    chip, core = lax.div(seq, 2), lax.rem(seq, 2)

    def device(chip_at, core_at):
        return {"seq": chip_at * 2 + core_at, "ch": z}

    def z_neighbour(direction):
        return {"seq": seq, "ch": lax.rem(z + (1 if direction == 0 else 7), 8)}

    barrier = pltpu.get_barrier_semaphore()
    for d in range(1, CHIPS):
        pl.semaphore_signal(barrier, inc=1, device_id=device(lax.rem(chip + d, CHIPS), core), device_id_type=MESH)
    pl.semaphore_signal(barrier, inc=1, device_id=device(chip, 1 - core), device_id_type=MESH)
    for direction in range(2):
        pl.semaphore_signal(barrier, inc=1, device_id=z_neighbour(direction), device_id_type=MESH)

    loads = [
        pltpu.make_async_copy(source, target, load_sem.at[at])
        for at, (source, target) in enumerate(
            [(decay_hbm, decay_buf), (k_hbm, k_buf), (v_hbm, v_buf), (residue_hbm, residue_buf), (q_hbm, q_buf)]
        )
    ]
    for load in loads:
        load.start()
    w_loads = {}
    for rd in (4, 5, 3, 2, 6, 1, 7, 0):
        columns = pl.ds(pl.multiple_of(lax.rem(z + rd, 8) * COLS, COLS), COLS)
        w_loads[rd] = pltpu.make_async_copy(w_hbm.at[:, columns], w_buf.at[rd], w_sem.at[rd])
        w_loads[rd].start()

    loads[0].wait()
    for j in range(8):
        rate[pl.ds(j, 16, stride=8), :] = decay_buf[pl.ds(128 * j, 128), :].T
    ratio[...] = jnp.exp(-rate[...])

    loads[1].wait()
    loads[2].wait()

    def carrier_rows(i, _):
        rows = pl.ds(pl.multiple_of(i * 16, 16), 16)
        product = (k_buf[rows, :].astype(F32) * v_buf[rows, :].astype(F32)).astype(BF16).astype(F32)
        for j in range(8):
            xs[pl.ds(i * 128 + j, 16, stride=8), :] = product[:, 128 * j : 128 * j + 128]
        return 0

    lax.fori_loop(0, ROWS // 16, carrier_rows, 0)

    def row(ref, t):
        return ref[pl.ds(pl.multiple_of(t * 8, 8), 8), :]

    def own_state(half):
        a = [row(ratio, half * 8 + n) for n in range(8)]
        a4 = [(s * s) * (s * s) for s in a]

        def four(i, state):
            x = [row(xs, 4 * i + r) for r in range(4)]
            return tuple(a4[n] * state[n] + (((a[n] * x[0] + x[1]) * a[n] + x[2]) * a[n] + x[3]) for n in range(8))

        state = lax.fori_loop(0, ROWS // 4, four, tuple(jnp.zeros((8, 128), F32) for _ in range(8)))
        for n in range(8):
            own[pl.ds(pl.multiple_of((half * 8 + n) * 8, 8), 8), :] = state[n]

    def half_rows(half):
        return pl.ds(pl.multiple_of(half * 64, 64), 64)

    def core_copy(half, at):
        return pltpu.make_async_remote_copy(
            src_ref=own.at[half_rows(half), :], dst_ref=other.at[half_rows(half), :],
            send_sem=core_send.at[at], recv_sem=core_recv.at[at], device_id=device(chip, 1 - core), device_id_type=MESH,
        )

    own_state(1 - core)
    pl.semaphore_wait(barrier, CHIPS - 1 + 1 + 2)
    first = core_copy(1 - core, 0)
    first.start()
    own_state(core)
    second = core_copy(core, 1)
    second.start()

    first.wait_recv()
    mine = half_rows(core)
    chunk = jnp.exp(rate[mine, :] * -float(ROWS))
    is_second = core == 1
    older = jnp.where(is_second, other[mine, :], own[mine, :])
    newer = jnp.where(is_second, own[mine, :], other[mine, :])
    total[...] = chunk * older + newer

    def total_copy(d):
        return pltpu.make_async_remote_copy(
            src_ref=total, dst_ref=totals.at[chip], send_sem=total_send.at[d], recv_sem=total_recv.at[chip],
            device_id=device(lax.rem(chip + d, CHIPS), core), device_id_type=MESH,
        )

    for d in range(CHIPS - 1, 0, -1):
        @pl.when(chip + d < CHIPS)
        def _():
            total_copy(d).start()

    loads[3].wait()
    for j in range(8):
        weight[pl.ds(j, 16, stride=8), :] = residue_buf[pl.ds(128 * j, 128), :].T
    weight[...] = weight[...] * jnp.sqrt(one_minus_exp(2.0 * rate[...]))

    for half in range(2):
        a = [row(ratio, half * 8 + n) for n in range(8)]
        w = [row(weight, half * 8 + n) for n in range(8)]

        def local_rows(i, state):
            for r in range(4):
                t = 4 * i + r
                x = row(xs, t)
                state = tuple(a[n] * state[n] + x for n in range(8))
                terms = [w[n] * state[n] for n in range(8)]
                y = ((terms[0] + terms[1]) + (terms[2] + terms[3])) + ((terms[4] + terms[5]) + (terms[6] + terms[7]))
                if half == 1:
                    y = y + row(ys, t)
                ys[pl.ds(pl.multiple_of(t * 8, 8), 8), :] = y
            return state

        lax.fori_loop(0, ROWS // 4, local_rows, tuple(jnp.zeros((8, 128), F32) for _ in range(8)))

    chip_decay = jnp.exp(rate[mine, :] * -float(2 * ROWS))

    def add_chip(p, state):
        pltpu.make_async_remote_copy(
            src_ref=total, dst_ref=totals.at[p], send_sem=total_send.at[0], recv_sem=total_recv.at[p],
            device_id=device(chip, 1 - core), device_id_type=MESH,
        ).wait_recv()
        return chip_decay * state + totals[p]

    carry[mine, :] = lax.fori_loop(0, chip, add_chip, jnp.zeros((64, 128), F32))
    carry_copy = pltpu.make_async_remote_copy(
        src_ref=carry.at[mine, :], dst_ref=carry.at[mine, :], send_sem=carry_send.at[0], recv_sem=carry_recv.at[0],
        device_id=device(chip, 1 - core), device_id_type=MESH,
    )
    carry_copy.start()
    second.wait_recv()
    loads[4].wait()
    carry_copy.wait_recv()

    before = jnp.where(is_second, jnp.exp(rate[...] * -float(ROWS)) * carry[...] + other[...], carry[...])
    own_carry = weight[...] * before

    def gate(block):
        start = own_carry * jnp.exp(rate[...] * -float(block * BLOCK))
        a = [row(ratio, n) for n in range(16)]

        def four(i, state):
            for r in range(4):
                t = block * BLOCK + 4 * i + r
                state = tuple(a[n] * state[n] for n in range(16))
                sums = [(state[4 * m] + state[4 * m + 1]) + (state[4 * m + 2] + state[4 * m + 3]) for m in range(4)]
                ys[pl.ds(pl.multiple_of(t * 8, 8), 8), :] = row(ys, t) + ((sums[0] + sums[1]) + (sums[2] + sums[3]))
            return state

        lax.fori_loop(0, BLOCK // 4, four, tuple(start[8 * n : 8 * n + 8] for n in range(16)))

        def sixteen(i, _):
            rows = pl.ds(pl.multiple_of(block * BLOCK + i * 16, 16), 16)
            for j in range(8):
                lanes = pl.ds(128 * j, 128)
                y = ys[pl.ds((block * BLOCK + i * 16) * 8 + j, 16, stride=8), :]
                gated[rows, lanes] = (q_buf[rows, lanes].astype(F32) * y).astype(BF16)
            return 0

        lax.fori_loop(0, BLOCK // 16, sixteen, 0)

    def rows_of(block):
        return pl.ds(block * BLOCK, BLOCK)

    def z_copy(direction, at):
        return pltpu.make_async_remote_copy(
            src_ref=sent.at[direction, at], dst_ref=received.at[direction, at],
            send_sem=z_send.at[direction, at], recv_sem=z_recv.at[direction, at],
            device_id=z_neighbour(direction), device_id_type=MESH,
        )

    def block_of(direction, block):
        return block if direction == 0 else (block + 2) % 4

    def relative(direction, block, step):
        return distance(block, step) if direction == 0 else 8 - distance(block, step)

    w_loads[4].wait()
    w_loads[5].wait()
    w_loads[3].wait()
    for block in (0, 2, 1, 3):
        gate(block)
        for direction in range(2):
            listed = block_of(direction, block)
            product = jnp.dot(gated[rows_of(block), :], w_buf[relative(direction, listed, 0)], preferred_element_type=F32)
            sent[direction, INDEX[listed, 0]] = product.astype(BF16)
            z_copy(direction, INDEX[listed, 0]).start()

    for rd in (2, 6, 1, 7, 0):
        w_loads[rd].wait()

    def products(k, _):
        rd = jnp.where(lax.rem(k, 2) == 0, 3 - lax.div(k, 2), 5 + lax.div(k, 2))
        for n in range(2):
            lanes = pl.ds(256 * n, 256)
            part[rd, :, lanes] = jnp.dot(gated[...], w_buf[rd, :, lanes], preferred_element_type=F32)
        return 0

    lax.fori_loop(0, 7, products, 0)

    for at, (listed, step) in enumerate(UNITS):
        if step == 0:
            continue
        for direction in range(2):
            block = block_of(direction, listed)
            previous = INDEX[listed, step - 1]
            z_copy(direction, previous).wait_recv()
            summed = part[relative(direction, listed, step), rows_of(block), :] + received[direction, previous].astype(F32)
            sent[direction, at] = summed.astype(BF16)
            z_copy(direction, at).start()

    outs = []
    for block in (0, 2, 1, 3):
        summed = part[0, rows_of(block), :]
        for direction in range(2):
            listed = block_of(direction, block)
            last = INDEX[listed, 3 if listed < 2 else 2]
            z_copy(direction, last).wait_recv()
            summed = summed + received[direction, last].astype(F32)
        out_buf[rows_of(block), :] = summed.astype(BF16)
        outs.append(pltpu.make_async_copy(out_buf.at[rows_of(block), :], out_hbm.at[rows_of(block), :], out_sem.at[block]))
        outs[-1].start()

    first.wait_send()
    second.wait_send()
    for d in range(1, CHIPS):
        @pl.when(chip + d < CHIPS)
        def _():
            total_copy(d).wait_send()
    carry_copy.wait_send()
    for direction in range(2):
        for at in range(len(UNITS)):
            z_copy(direction, at).wait_send()
    for out in outs:
        out.wait()


def per_device(query_proj, key_projected, value_projected, mode_decay_speed, residue, out_weight):
    vmem, dma = pltpu.VMEM, pltpu.SemaphoreType.DMA
    units = len(UNITS)
    return pl.pallas_call(
        kernel,
        out_shape=jax.ShapeDtypeStruct((ROWS, COLS), BF16),
        in_specs=[pl.BlockSpec(memory_space=pl.ANY)] * 6,
        out_specs=pl.BlockSpec(memory_space=pl.ANY),
        scratch_shapes=[
            vmem((ROWS, WIDTH), BF16), vmem((ROWS, WIDTH), BF16), vmem((ROWS, WIDTH), BF16),
            vmem((WIDTH, 16), F32), vmem((WIDTH, 16), F32), vmem((8, WIDTH, COLS), BF16),
            vmem((128, 128), F32), vmem((128, 128), F32), vmem((128, 128), F32),
            vmem((ROWS * 8, 128), F32), vmem((ROWS * 8, 128), F32),
            vmem((128, 128), F32), vmem((128, 128), F32), vmem((64, 128), F32), vmem((CHIPS, 64, 128), F32),
            vmem((128, 128), F32), vmem((ROWS, WIDTH), BF16), vmem((8, ROWS, COLS), F32),
            vmem((2, units, BLOCK, COLS), BF16), vmem((2, units, BLOCK, COLS), BF16), vmem((ROWS, COLS), BF16),
            dma((5,)), dma((8,)), dma((2,)), dma((2,)), dma((CHIPS,)), dma((CHIPS,)), dma((1,)), dma((1,)),
            dma((2, units)), dma((2, units)), dma((4,)),
        ],
        compiler_params=pltpu.CompilerParams(collective_id=0, has_side_effects=True, vmem_limit_bytes=48 << 20),
        name="hyena",
    )(query_proj, key_projected, value_projected, mode_decay_speed, residue, out_weight)


def solution(mesh):
    return jax.shard_map(
        per_device,
        mesh=mesh,
        in_specs=(P("seq", "ch"), P("seq", "ch"), P("seq", "ch"), P("ch", None), P("ch", None), P("ch", None)),
        out_specs=P("seq", "ch"),
        check_vma=False,
    )
```

profile of v0, /device:TPU:6, one launch (start us, length us, event | category | flops | bytes accessed | tf_op | source)
XLA Modules:
  0.0 51.2 jit_solution(4981021618929136945)
XLA Ops:
  0.0 1.0 %copy.7.decay_hbm = f32[1024,16]{1,0:T(8,128)S(1)} copy(f32[1024,16]{0,1:T(8,128)} %param.9) | data formatting | bytes 131072 | tf_op args[3]
  1.0 1.0 %copy.8.residue_hbm = f32[1024,16]{1,0:T(8,128)S(1)} copy(f32[1024,16]{0,1:T(8,128)} %param.10) | data formatting | bytes 131072 | tf_op args[4]
  2.1 0.0 copy-start
  2.1 1.0 %copy-done = bf16[256,1024]{1,0:T(8,128)(2,1)S(1)} copy-done((bf16[256,1024]{1,0:T(8,128)(2,1)S(1)}, bf16[256,1024]{1,0:T(8,128)(2,1)}, u32[]{:S(2)}) %copy-start) | copy-done | bytes 524312
  3.1 0.0 copy-start.1
  3.1 1.0 %copy-done.1 = bf16[256,1024]{1,0:T(8,128)(2,1)S(1)} copy-done((bf16[256,1024]{1,0:T(8,128)(2,1)S(1)}, bf16[256,1024]{1,0:T(8,128)(2,1)}, u32[]{:S(2)}) %copy-start.1) | copy-done | bytes 524312
  4.2 0.0 copy-start.2
  4.2 1.0 %copy-done.2 = bf16[256,1024]{1,0:T(8,128)(2,1)S(1)} copy-done((bf16[256,1024]{1,0:T(8,128)(2,1)S(1)}, bf16[256,1024]{1,0:T(8,128)(2,1)}, u32[]{:S(2)}) %copy-start.2) | copy-done | bytes 524312
  5.2 45.2 %hyena.1 = bf16[256,512]{1,0:T(8,128)(2,1)S(1)} custom-call(bf16[256,1024]{1,0:T(8,128)(2,1)S(1)} %copy-done, bf16[256,1024]{1,0:T(8,128)(2,1)S(1)} %copy-done.1, bf16[256,1024]{1,0:T(8,128)(2,1)S(1)} %copy-done.2, f32[1024,16]{1,0:T(8,128)S(1)} %copy.7.decay_hbm, f32[1024,16]{1,0:T(8,128)S(1)} %copy.8.residue_hbm, bf16[1024,4096]{1,0:T(8,128)(2,1)} %w_hbm.1), custom_call_target="tpu_custom_call" | custom-call | tf_op jit(solution)/shard_map/hyena/pallas_call | solution.py:286
  50.5 0.7 %copy.10 = bf16[256,512]{1,0:T(8,128)(2,1)} copy(bf16[256,512]{1,0:T(8,128)(2,1)S(1)} %hyena.1) | data formatting | bytes 524288
Async XLA Ops:
  2.1 1.0 %copy-start = (bf16[256,1024]{1,0:T(8,128)(2,1)S(1)}, bf16[256,1024]{1,0:T(8,128)(2,1)}, u32[]{:S(2)}) copy-start(bf16[256,1024]{1,0:T(8,128)(2,1)} %q_hbm.1) | copy-start | bytes 1572868
  3.1 1.0 %copy-start.1 = (bf16[256,1024]{1,0:T(8,128)(2,1)S(1)}, bf16[256,1024]{1,0:T(8,128)(2,1)}, u32[]{:S(2)}) copy-start(bf16[256,1024]{1,0:T(8,128)(2,1)} %k_hbm.1) | copy-start | bytes 1572868
  4.2 1.0 %copy-start.2 = (bf16[256,1024]{1,0:T(8,128)(2,1)S(1)}, bf16[256,1024]{1,0:T(8,128)(2,1)}, u32[]{:S(2)}) copy-start(bf16[256,1024]{1,0:T(8,128)(2,1)} %v_hbm.1) | copy-start | bytes 1572868
where the time goes:
time: 51.8 us; the launch traced here: 51.2 us
  Pallas kernels  45.2 us (87%)
  local copies, waits for them, and re-layouts  5.9 us (11%)
    pallas_call x1, Pallas kernels, per_device(): pl.pallas_call(kernel, out_shape=jax.ShapeDtypeStruct((ROWS, COLS), BF16)...  45.2 us
    unnamed x9, local copies, waits for them, and re-layouts  5.9 us

commit v1 on v0

v1 whole, which is shorter than its diff:
```python
import jax
import jax.numpy as jnp
from jax import lax
from jax.experimental import pallas as pl
from jax.experimental.pallas import tpu as pltpu
from jax.sharding import PartitionSpec as P

MESH = pl.DeviceIdType.MESH
F32, BF16 = jnp.float32, jnp.bfloat16

ROWS = 256
WIDTH = 1024
COLS = 512
BLOCK = 64
SIDE = 4

HOPS = ((4, 4, 3, 3), (3, 3, 4, 4))
ORDER = (
    ((0, 0), (2, 0), (1, 0), (3, 0), (0, 1), (1, 1), (2, 1), (3, 1), (0, 2), (1, 2), (2, 2), (3, 2), (0, 3), (1, 3)),
    ((0, 0), (2, 0), (1, 0), (3, 0), (2, 1), (0, 1), (3, 1), (1, 1), (2, 2), (3, 2), (0, 2), (1, 2), (2, 3), (3, 3)),
)
UNITS = len(ORDER[0])
INDEX = tuple({unit: at for at, unit in enumerate(order)} for order in ORDER)


def relative(direction, block, step):
    left_over = HOPS[direction][block] - step
    return left_over if direction == 0 else 8 - left_over


def one_minus_exp(u):
    series = jnp.ones_like(u)
    for order in range(8, 1, -1):
        series = 1.0 - u * series * (1.0 / order)
    return jnp.where(u < 0.25, u * series, 1.0 - jnp.exp(-u))


def kernel(
    q_hbm, k_hbm, v_hbm, decay_hbm, residue_hbm, w_hbm, out,
    q_buf, k_buf, v_buf, decay_buf, residue_buf, w_buf,
    rate, ratio, weight, xs, ys, own, other, total, row_total, totals, carry, gated, part, sent, received,
    load_sem, w_sem, core_send, core_recv, total_send, total_recv, carry_send, carry_recv, z_send, z_recv,
):
    seq, z = lax.axis_index("seq"), lax.axis_index("ch")
    chip, core = lax.div(seq, 2), lax.rem(seq, 2)
    at_x, at_y = lax.div(chip, SIDE), lax.rem(chip, SIDE)
    is_second = core == 1

    def device(x, y, core_at):
        return {"seq": (x * SIDE + y) * 2 + core_at, "ch": z}

    def z_neighbour(direction):
        return {"seq": seq, "ch": lax.rem(z + (1 if direction == 0 else 7), 8)}

    other_core = device(at_x, at_y, 1 - core)

    barrier = pltpu.get_barrier_semaphore()
    for d in range(1, SIDE):
        for partner in (device(lax.rem(at_x + d, SIDE), at_y, core), device(at_x, lax.rem(at_y + d, SIDE), core)):
            pl.semaphore_signal(barrier, inc=1, device_id=partner, device_id_type=MESH)
    for partner in (other_core, z_neighbour(0), z_neighbour(1)):
        pl.semaphore_signal(barrier, inc=1, device_id=partner, device_id_type=MESH)

    loads = [
        pltpu.make_async_copy(source, target, load_sem.at[at])
        for at, (source, target) in enumerate(
            [(decay_hbm, decay_buf), (k_hbm, k_buf), (v_hbm, v_buf), (residue_hbm, residue_buf), (q_hbm, q_buf)]
        )
    ]
    for load in loads:
        load.start()

    loads[0].wait()
    for j in range(8):
        rate[pl.ds(j, 16, stride=8), :] = decay_buf[:, pl.ds(128 * j, 128)]
    ratio[...] = jnp.exp(-rate[...])

    loads[1].wait()
    loads[2].wait()
    w_loads = {}
    for rd in (4, 5, 3, 2, 6, 1, 7, 0):
        columns = pl.ds(pl.multiple_of(lax.rem(z + rd, 8) * COLS, COLS), COLS)
        w_loads[rd] = pltpu.make_async_copy(w_hbm.at[:, columns], w_buf.at[rd], w_sem.at[rd])
        w_loads[rd].start()

    def carrier_rows(i, _):
        rows = pl.ds(pl.multiple_of(i * 16, 16), 16)
        product = (k_buf[rows, :].astype(F32) * v_buf[rows, :].astype(F32)).astype(BF16).astype(F32)
        for j in range(8):
            xs[pl.ds(i * 128 + j, 16, stride=8), :] = product[:, 128 * j : 128 * j + 128]
        return 0

    lax.fori_loop(0, ROWS // 16, carrier_rows, 0)

    def row(ref, t):
        return ref[pl.ds(pl.multiple_of(t * 8, 8), 8), :]

    def modes(ref, half):
        return [row(ref, half * 8 + n) for n in range(8)]

    def own_state(half):
        a = modes(ratio, half)
        a4 = [(s * s) * (s * s) for s in a]

        def four(i, state):
            x = [row(xs, 4 * i + r) for r in range(4)]
            return tuple(a4[n] * state[n] + (((a[n] * x[0] + x[1]) * a[n] + x[2]) * a[n] + x[3]) for n in range(8))

        state = lax.fori_loop(0, ROWS // 4, four, tuple(jnp.zeros((8, 128), F32) for _ in range(8)))
        for n in range(8):
            own[pl.ds(pl.multiple_of((half * 8 + n) * 8, 8), 8), :] = state[n]

    def half_rows(half):
        return pl.ds(pl.multiple_of(half * 64, 64), 64)

    mine, theirs = half_rows(core), half_rows(1 - core)

    def core_copy(half, at):
        return pltpu.make_async_remote_copy(
            src_ref=own.at[half_rows(half), :], dst_ref=other.at[half_rows(half), :],
            send_sem=core_send.at[at], recv_sem=core_recv.at[at], device_id=other_core, device_id_type=MESH,
        )

    own_state(1 - core)
    pl.semaphore_wait(barrier, 2 * (SIDE - 1) + 3)
    first = core_copy(1 - core, 0)
    first.start()
    own_state(core)
    second = core_copy(core, 1)
    second.start()

    device_decay = jnp.exp(rate[mine, :] * -float(ROWS))
    chip_decay = jnp.exp(rate[mine, :] * -float(2 * ROWS))
    first.wait_recv()
    older = jnp.where(is_second, other[mine, :], own[mine, :])
    newer = jnp.where(is_second, own[mine, :], other[mine, :])
    total[...] = (device_decay * older + newer).astype(BF16)

    def y_copy(d):
        return pltpu.make_async_remote_copy(
            src_ref=total, dst_ref=totals.at[at_y], send_sem=total_send.at[d], recv_sem=total_recv.at[at_y],
            device_id=device(at_x, lax.rem(at_y + d, SIDE), core), device_id_type=MESH,
        )

    def x_copies(act):
        for d in range(SIDE - 1, 0, -1):
            @pl.when(at_x + d < SIDE)
            def _():
                act(pltpu.make_async_remote_copy(
                    src_ref=row_total, dst_ref=totals.at[SIDE + at_x],
                    send_sem=total_send.at[SIDE + d], recv_sem=total_recv.at[SIDE + at_x],
                    device_id=device(at_x + d, at_y, core), device_id_type=MESH,
                ))

    def landed(at):
        return pltpu.make_async_remote_copy(
            src_ref=total, dst_ref=totals.at[at], send_sem=total_send.at[0], recv_sem=total_recv.at[at],
            device_id=other_core, device_id_type=MESH,
        )

    for d in (2, 3, 1):
        y_copy(d).start()
    totals[at_y] = total[...]

    loads[3].wait()
    for j in range(8):
        weight[pl.ds(j, 16, stride=8), :] = residue_buf[:, pl.ds(128 * j, 128)]
    weight[...] = weight[...] * jnp.sqrt(one_minus_exp(2.0 * rate[...]))

    def local(half):
        a, w = modes(ratio, half), modes(weight, half)

        def four(i, state):
            for r in range(4):
                t = 4 * i + r
                x = row(xs, t)
                state = tuple(a[n] * state[n] + x for n in range(8))
                terms = [w[n] * state[n] for n in range(8)]
                y = ((terms[0] + terms[1]) + (terms[2] + terms[3])) + ((terms[4] + terms[5]) + (terms[6] + terms[7]))
                if half == 1:
                    y = y + row(ys, t)
                ys[pl.ds(pl.multiple_of(t * 8, 8), 8), :] = y
            return state

        lax.fori_loop(0, ROWS // 4, four, tuple(jnp.zeros((8, 128), F32) for _ in range(8)))

    local(0)

    for d in (1, 3, 2):
        landed(lax.rem(at_y + d, SIDE)).wait_recv()
    whole = partial = jnp.zeros((64, 128), F32)
    for y in range(SIDE):
        value = totals[y].astype(F32)
        whole = chip_decay * whole + value
        partial = jnp.where(y < at_y, chip_decay * partial + value, partial)
    row_total[...] = whole.astype(BF16)
    x_copies(lambda copy: copy.start())
    local(1)

    row_decay = jnp.exp(rate[mine, :] * -float(2 * SIDE * ROWS))

    def add_row(x, state):
        landed(SIDE + x).wait_recv()
        return row_decay * state + totals[SIDE + x].astype(F32)

    rows_before = lax.fori_loop(0, at_x, add_row, jnp.zeros((64, 128), F32))
    carry[mine, :] = jnp.exp(rate[mine, :] * (-float(2 * ROWS) * at_y.astype(F32))) * rows_before + partial
    carry_copy = pltpu.make_async_remote_copy(
        src_ref=carry.at[mine, :], dst_ref=carry.at[mine, :], send_sem=carry_send.at[0], recv_sem=carry_recv.at[0],
        device_id=other_core, device_id_type=MESH,
    )
    carry_copy.start()

    def weighted(rows):
        before = jnp.exp(rate[rows, :] * -float(ROWS)) * carry[rows, :] + other[rows, :]
        return weight[rows, :] * jnp.where(is_second, before, carry[rows, :])

    def add_carried(half, start, first_row, count):
        a = modes(ratio, half)

        def four(i, state):
            for r in range(4):
                t = first_row + 4 * i + r
                state = tuple(a[n] * state[n] for n in range(8))
                sums = [(state[4 * m] + state[4 * m + 1]) + (state[4 * m + 2] + state[4 * m + 3]) for m in range(2)]
                ys[pl.ds(pl.multiple_of(t * 8, 8), 8), :] = row(ys, t) + (sums[0] + sums[1])
            return state

        lax.fori_loop(0, count // 4, four, tuple(start[8 * n : 8 * n + 8] for n in range(8)))

    add_carried(core, weighted(mine), 0, ROWS)
    second.wait_recv()
    loads[4].wait()
    carry_copy.wait_recv()
    own_carry = weighted(theirs)

    def gate(block):
        add_carried(1 - core, own_carry * jnp.exp(rate[theirs, :] * -float(block * BLOCK)), block * BLOCK, BLOCK)

        def sixteen(i, _):
            rows = pl.ds(pl.multiple_of(block * BLOCK + i * 16, 16), 16)
            for j in range(8):
                lanes = pl.ds(128 * j, 128)
                y = ys[pl.ds((block * BLOCK + i * 16) * 8 + j, 16, stride=8), :]
                gated[rows, lanes] = (q_buf[rows, lanes].astype(F32) * y).astype(BF16)
            return 0

        lax.fori_loop(0, BLOCK // 16, sixteen, 0)

    def rows_of(block):
        return pl.ds(block * BLOCK, BLOCK)

    def z_copy(direction, at):
        return pltpu.make_async_remote_copy(
            src_ref=sent.at[direction, at], dst_ref=received.at[direction, at],
            send_sem=z_send.at[direction, at], recv_sem=z_recv.at[direction, at],
            device_id=z_neighbour(direction), device_id_type=MESH,
        )

    for rd in (4, 5, 3):
        w_loads[rd].wait()
    for at in range(4):
        block = ORDER[0][at][0]
        gate(block)
        for direction in range(2):
            product = jnp.dot(gated[rows_of(block), :], w_buf[relative(direction, block, 0)], preferred_element_type=F32)
            sent[direction, at] = product.astype(BF16)
            z_copy(direction, at).start()

    def products(k, _):
        rd = jnp.where(lax.rem(k, 2) == 0, 3 - lax.div(k, 2), 5 + lax.div(k, 2))
        for n in range(2):
            lanes = pl.ds(256 * n, 256)
            part[rd, :, lanes] = jnp.dot(gated[...], w_buf[rd, :, lanes], preferred_element_type=F32)
        return 0

    for rd in (2, 6):
        w_loads[rd].wait()
    lax.fori_loop(0, 4, products, 0)

    for at in range(4, UNITS):
        if at == 8:
            for rd in (1, 7, 0):
                w_loads[rd].wait()
            lax.fori_loop(4, 7, products, 0)
        for direction in range(2):
            block, step = ORDER[direction][at]
            previous = INDEX[direction][block, step - 1]
            z_copy(direction, previous).wait_recv()
            summed = part[relative(direction, block, step), rows_of(block), :] + received[direction, previous].astype(F32)
            sent[direction, at] = summed.astype(BF16)
            z_copy(direction, at).start()

    for block in (0, 2, 1, 3):
        summed = part[0, rows_of(block), :]
        for direction in range(2):
            last = INDEX[direction][block, HOPS[direction][block] - 1]
            z_copy(direction, last).wait_recv()
            summed = summed + received[direction, last].astype(F32)
        out[rows_of(block), :] = summed.astype(BF16)

    first.wait_send()
    second.wait_send()
    for d in range(1, SIDE):
        y_copy(d).wait_send()
    x_copies(lambda copy: copy.wait_send())
    carry_copy.wait_send()
    for direction in range(2):
        for at in range(UNITS):
            z_copy(direction, at).wait_send()


def per_device(query_proj, key_projected, value_projected, mode_decay_speed, residue, out_weight):
    vmem, dma = pltpu.VMEM, pltpu.SemaphoreType.DMA
    operands = (query_proj, key_projected, value_projected, mode_decay_speed.T, residue.T, out_weight)
    return pl.pallas_call(
        kernel,
        out_shape=jax.ShapeDtypeStruct((ROWS, COLS), BF16),
        in_specs=[pl.BlockSpec(memory_space=pltpu.HBM)] * 6,
        out_specs=pl.BlockSpec(memory_space=pltpu.VMEM),
        scratch_shapes=[
            vmem((ROWS, WIDTH), BF16), vmem((ROWS, WIDTH), BF16), vmem((ROWS, WIDTH), BF16),
            vmem((16, WIDTH), F32), vmem((16, WIDTH), F32), vmem((8, WIDTH, COLS), BF16),
            vmem((128, 128), F32), vmem((128, 128), F32), vmem((128, 128), F32),
            vmem((ROWS * 8, 128), F32), vmem((ROWS * 8, 128), F32),
            vmem((128, 128), F32), vmem((128, 128), F32),
            vmem((64, 128), BF16), vmem((64, 128), BF16), vmem((2 * SIDE, 64, 128), BF16),
            vmem((128, 128), F32), vmem((ROWS, WIDTH), BF16), vmem((8, ROWS, COLS), F32),
            vmem((2, UNITS, BLOCK, COLS), BF16), vmem((2, UNITS, BLOCK, COLS), BF16),
            dma((5,)), dma((8,)), dma((2,)), dma((2,)), dma((2 * SIDE,)), dma((2 * SIDE,)), dma((1,)), dma((1,)),
            dma((2, UNITS)), dma((2, UNITS)),
        ],
        compiler_params=pltpu.CompilerParams(collective_id=0, has_side_effects=True, vmem_limit_bytes=48 << 20),
        name="hyena",
    )(*(pltpu.with_memory_space_constraint(operand, pltpu.HBM) for operand in operands))


def solution(mesh):
    return jax.shard_map(
        per_device,
        mesh=mesh,
        in_specs=(P("seq", "ch"), P("seq", "ch"), P("seq", "ch"), P("ch", None), P("ch", None), P("ch", None)),
        out_specs=P("seq", "ch"),
        check_vma=False,
    )
```

time: 51.8 us -> 41.2 us (0.80); the launches traced: 51.2 us -> 41.1 us
  local copies, waits for them, and re-layouts: 5.9 us -> 0.71 us
  Pallas kernels: 45.2 us -> 40.4 us
    unnamed x9 -> x1, local copies, waits for them, and re-layouts: 5.9 us -> 0.71 us
    pallas_call x1, Pallas kernels: 45.2 us -> 40.4 us  [per_device(): pl.pallas_call(kernel, out_shape=jax.ShapeDtypeStruct((ROWS, COLS), BF16)...]
where the time goes in v1:
time: 41.2 us; the launch traced here: 41.1 us
  Pallas kernels  40.4 us (98%)
  local copies, waits for them, and re-layouts  0.71 us (2%)
    pallas_call x1, Pallas kernels, per_device(): pl.pallas_call(kernel, out_shape=jax.ShapeDtypeStruct((ROWS, COLS), BF16)...  40.4 us

profile of v1, /device:TPU:6, one launch (start us, length us, event | category | flops | bytes accessed | tf_op | source)
XLA Modules:
  0.0 41.1 jit_solution(12637413724024332826)
XLA Ops:
  0.0 40.4 %hyena.1 = bf16[256,512]{1,0:T(8,128)(2,1)S(1)} custom-call(bf16[256,1024]{1,0:T(8,128)(2,1)} %q_hbm.1, bf16[256,1024]{1,0:T(8,128)(2,1)} %k_hbm.1, bf16[256,1024]{1,0:T(8,128)(2,1)} %v_hbm.1, f32[16,1024]{1,0:T(8,128)} %bitcast.2, f32[16,1024]{1,0:T(8,128)} %bitcast.3, bf16[1024,4096]{1,0:T(8,128)(2,1)} %w_hbm.1), custom_call_target="tpu_custom_call" | custom-call | tf_op jit(solution)/shard_map/hyena/pallas_call | solution.py:316
  40.4 0.7 %copy.8 = bf16[256,512]{1,0:T(8,128)(2,1)} copy(bf16[256,512]{1,0:T(8,128)(2,1)S(1)} %hyena.1) | data formatting | bytes 524288

commit v2 on v1

v2 whole, which is shorter than its diff:
```python
import jax
import jax.numpy as jnp
from jax import lax
from jax.experimental import pallas as pl
from jax.experimental.pallas import tpu as pltpu
from jax.sharding import PartitionSpec as P

MESH = pl.DeviceIdType.MESH
F32, BF16 = jnp.float32, jnp.bfloat16

ROWS = 256
WIDTH = 1024
COLS = 512
BLOCK = 64
STEP = 8
SIDE = 4

HOPS = ((4, 4, 3, 3), (3, 3, 4, 4))
ORDER = (
    ((0, 0), (2, 0), (1, 0), (3, 0), (0, 1), (1, 1), (2, 1), (3, 1), (0, 2), (1, 2), (2, 2), (3, 2), (0, 3), (1, 3)),
    ((0, 0), (2, 0), (1, 0), (3, 0), (2, 1), (0, 1), (3, 1), (1, 1), (2, 2), (3, 2), (0, 2), (1, 2), (2, 3), (3, 3)),
)
UNITS = len(ORDER[0])
INDEX = tuple({unit: at for at, unit in enumerate(order)} for order in ORDER)


def relative(direction, block, step):
    left_over = HOPS[direction][block] - step
    return left_over if direction == 0 else 8 - left_over


def one_minus_exp(u):
    series = jnp.ones_like(u)
    for order in range(8, 1, -1):
        series = 1.0 - u * series * (1.0 / order)
    return jnp.where(u < 0.25, u * series, 1.0 - jnp.exp(-u))


def kernel(
    q_hbm, k_hbm, v_hbm, decay_hbm, residue_hbm, w_hbm, out,
    q_buf, k_buf, v_buf, decay_buf, residue_buf, w_buf,
    rate, ratio, ratio_step, weight, decays, starts, taps, kept, xs, ys, own, states, row_total, row_totals, prefixes, before, sent_before, gated, part, sent, received,
    load_sem, w_sem, state_send, state_recv, row_send, row_recv, core_send, core_recv, z_send, z_recv,
):
    seq, z = lax.axis_index("seq"), lax.axis_index("ch")
    chip, core = lax.div(seq, 2), lax.rem(seq, 2)
    at_x, at_y = lax.div(chip, SIDE), lax.rem(chip, SIDE)
    is_second = core == 1

    def device(x, y, core_at):
        return {"seq": (x * SIDE + y) * 2 + core_at, "ch": z}

    def z_neighbour(direction):
        return {"seq": seq, "ch": lax.rem(z + (1 if direction == 0 else 7), 8)}

    other_core = device(at_x, at_y, 1 - core)

    loads = [
        pltpu.make_async_copy(source, target, load_sem.at[at])
        for at, (source, target) in enumerate(
            [(decay_hbm, decay_buf), (k_hbm, k_buf), (v_hbm, v_buf), (residue_hbm, residue_buf), (q_hbm, q_buf)]
        )
    ]
    for load in loads:
        load.start()

    barrier = pltpu.get_barrier_semaphore()
    def greet(partner):
        pl.semaphore_signal(barrier, inc=1, device_id=partner, device_id_type=MESH)

    greet(other_core)
    greet(z_neighbour(0))
    greet(z_neighbour(1))

    @pl.when(is_second)
    def _():
        for d in range(1, SIDE):
            near = lax.rem(at_y + d, SIDE)
            for partner in (device(lax.rem(at_x + d, SIDE), at_y, 1), device(at_x, near, 1), device(at_x, near, 0)):
                greet(partner)

    loads[0].wait()
    for j in range(8):
        rate[pl.ds(j, 16, stride=8), :] = decay_buf[:, pl.ds(128 * j, 128)]
    ratio[...] = jnp.exp(-rate[...])
    ratio_step[...] = jnp.exp(-float(STEP) * rate[...])

    loads[1].wait()
    loads[2].wait()
    w_loads = {}
    for rd in (4, 5, 3, 2, 6, 1, 7, 0):
        columns = pl.ds(pl.multiple_of(lax.rem(z + rd, 8) * COLS, COLS), COLS)
        w_loads[rd] = pltpu.make_async_copy(w_hbm.at[:, columns], w_buf.at[rd], w_sem.at[rd])
        w_loads[rd].start()

    def carrier_rows(i, _):
        rows = pl.ds(pl.multiple_of(i * 16, 16), 16)
        product = (k_buf[rows, :].astype(F32) * v_buf[rows, :].astype(F32)).astype(BF16).astype(F32)
        for j in range(8):
            xs[pl.ds(i * 128 + j, 16, stride=8), :] = product[:, 128 * j : 128 * j + 128]
        return 0

    lax.fori_loop(0, ROWS // 16, carrier_rows, 0)

    def row(ref, t):
        return ref[pl.ds(pl.multiple_of(t * 8, 8), 8), :]

    def modes(ref, half):
        return [row(ref, half * 8 + n) for n in range(8)]

    def own_state(half):
        a, a_step = modes(ratio, half), modes(ratio_step, half)

        def step(i, state):
            x = [row(xs, STEP * i + r) for r in range(STEP)]
            after = []
            for n in range(8):
                kept[pl.ds(pl.multiple_of((i * 16 + half * 8 + n) * 8, 8), 8), :] = state[n]
                added = x[0]
                for r in range(1, STEP):
                    added = added * a[n] + x[r]
                after.append(a_step[n] * state[n] + added)
            return tuple(after)

        state = lax.fori_loop(0, ROWS // STEP, step, tuple(jnp.zeros((8, 128), F32) for _ in range(8)))
        own[half] = jnp.concatenate(state, axis=0).astype(BF16)

    def state_copy(half, d):
        return pltpu.make_async_remote_copy(
            src_ref=own.at[half], dst_ref=states.at[2 * at_y + core, half],
            send_sem=state_send.at[half, d], recv_sem=state_recv.at[2 * at_y + core, half],
            device_id=device(at_x, lax.rem(at_y + d, SIDE), 1), device_id_type=MESH,
        )

    def state_copies(half, act):
        for d in (2, 3, 1):
            act(state_copy(half, d))

        @pl.when(jnp.logical_not(is_second))
        def _():
            act(state_copy(half, 0))

    own_state(0)
    @pl.when(is_second)
    def _():
        pl.semaphore_wait(barrier, 3 * (SIDE - 1))

    @pl.when(jnp.logical_not(is_second))
    def _():
        pl.semaphore_wait(barrier, SIDE + 2)

    state_copies(0, lambda copy: copy.start())
    own_state(1)
    state_copies(1, lambda copy: copy.start())

    def row_copies(half, act):
        for d in range(SIDE - 1, 0, -1):
            @pl.when(at_x + d < SIDE)
            def _():
                act(pltpu.make_async_remote_copy(
                    src_ref=row_total.at[half], dst_ref=row_totals.at[at_x, half],
                    send_sem=row_send.at[d, half], recv_sem=row_recv.at[at_x, half],
                    device_id=device(at_x + d, at_y, 1), device_id_type=MESH,
                ))

    loads[3].wait()
    for j in range(8):
        weight[pl.ds(j, 16, stride=8), :] = residue_buf[:, pl.ds(128 * j, 128)]
    weight[...] = weight[...] * jnp.sqrt(one_minus_exp(2.0 * rate[...]))
    decays[0] = jnp.exp(-float(ROWS) * rate[...])
    decays[1] = jnp.exp(-float(2 * SIDE * ROWS) * rate[...])
    for core_at in range(2):
        decays[2 + core_at] = jnp.exp(rate[...] * (-float(ROWS) * (2 * at_y + core_at).astype(F32)))
    for block in range(ROWS // BLOCK):
        starts[block] = weight[...] * jnp.exp(rate[...] * -float(block * BLOCK))

    power = weight[...]
    for k in range(STEP):
        tap = power[0:8]
        for n in range(1, 16):
            tap = tap + power[8 * n : 8 * n + 8]
        taps[8 * k : 8 * k + 8, :] = tap
        power = power * ratio[...]

    def local(i, _):
        f = [row(taps, k) for k in range(STEP)]
        x = [row(xs, STEP * i + r) for r in range(STEP)]
        for r in range(STEP):
            y = f[r] * x[0]
            for k in range(1, r + 1):
                y = y + f[r - k] * x[k]
            ys[pl.ds(pl.multiple_of((STEP * i + r) * 8, 8), 8), :] = y
        rows = pl.ds(pl.multiple_of(i * 128, 128), 128)
        kept[rows, :] = kept[rows, :] * weight[...]
        return 0

    lax.fori_loop(0, ROWS // STEP, local, 0)

    @pl.when(is_second)
    def _():
        states[2 * at_y + 1, 0] = own[0]
        states[2 * at_y + 1, 1] = own[1]
        prefixes[0] = jnp.zeros((128, 128), F32)

        def wait_state(i, _):
            sender = lax.rem(2 * at_y + 2 + i, 2 * SIDE)
            for half in range(2):
                pltpu.make_async_remote_copy(
                    src_ref=own.at[half], dst_ref=states.at[sender, half], send_sem=state_send.at[half, 0],
                    recv_sem=state_recv.at[sender, half], device_id=other_core, device_id_type=MESH,
                ).wait_recv()
            return 0

        lax.fori_loop(0, 2 * SIDE - 1, wait_state, 0)
        for half in range(2):
            rows = pl.ds(64 * half, 64)
            device_decay = decays[0, rows, :]
            whole = states[0, half].astype(F32)
            for at in range(1, 2 * SIDE):
                prefixes[at, rows, :] = whole
                whole = device_decay * whole + states[at, half].astype(F32)
            row_total[half] = whole.astype(BF16)
            row_copies(half, lambda copy: copy.start())

    def core_copy(half):
        return pltpu.make_async_remote_copy(
            src_ref=sent_before.at[half], dst_ref=before.at[half], send_sem=core_send.at[half], recv_sem=core_recv.at[half],
            device_id=other_core, device_id_type=MESH,
        )

    @pl.when(is_second)
    def _():
        for half in range(2):
            rows = pl.ds(64 * half, 64)
            row_decay = decays[1, rows, :]

            def add_row(x, state):
                pltpu.make_async_remote_copy(
                    src_ref=row_total.at[half], dst_ref=row_totals.at[x, half], send_sem=row_send.at[0, half],
                    recv_sem=row_recv.at[x, half], device_id=other_core, device_id_type=MESH,
                ).wait_recv()
                return row_decay * state + row_totals[x, half].astype(F32)

            rows_before = lax.fori_loop(0, at_x, add_row, jnp.zeros((64, 128), F32))
            sent_before[half] = decays[2, rows, :] * rows_before + prefixes[2 * at_y, rows, :]
            core_copy(half).start()
            before[half] = decays[3, rows, :] * rows_before + prefixes[2 * at_y + 1, rows, :]

    @pl.when(jnp.logical_not(is_second))
    def _():
        core_copy(0).wait_recv()
        core_copy(1).wait_recv()

    loads[4].wait()
    def gate(block):
        a = modes(ratio, 0) + modes(ratio, 1)

        def step(i, carried):
            at = block * (BLOCK // STEP) + i
            state = tuple(carried[n] + row(kept, at * 16 + n) for n in range(16))
            for r in range(STEP):
                t = STEP * at + r
                state = tuple(a[n] * state[n] for n in range(16))
                sums = [(state[4 * m] + state[4 * m + 1]) + (state[4 * m + 2] + state[4 * m + 3]) for m in range(4)]
                ys[pl.ds(pl.multiple_of(t * 8, 8), 8), :] = row(ys, t) + ((sums[0] + sums[1]) + (sums[2] + sums[3]))
            return tuple(carried[n] * row(ratio_step, n) for n in range(16))

        lax.fori_loop(0, BLOCK // STEP, step, tuple(
            before[n // 8, 8 * (n % 8) : 8 * (n % 8) + 8, :] * starts[block, 8 * n : 8 * n + 8, :] for n in range(16)
        ))

        def sixteen(i, _):
            rows = pl.ds(pl.multiple_of(block * BLOCK + i * 16, 16), 16)
            for j in range(8):
                lanes = pl.ds(128 * j, 128)
                y = ys[pl.ds((block * BLOCK + i * 16) * 8 + j, 16, stride=8), :]
                gated[rows, lanes] = (q_buf[rows, lanes].astype(F32) * y).astype(BF16)
            return 0

        lax.fori_loop(0, BLOCK // 16, sixteen, 0)

    def rows_of(block):
        return pl.ds(block * BLOCK, BLOCK)

    def z_copy(direction, at):
        return pltpu.make_async_remote_copy(
            src_ref=sent.at[direction, at], dst_ref=received.at[direction, at],
            send_sem=z_send.at[direction, at], recv_sem=z_recv.at[direction, at],
            device_id=z_neighbour(direction), device_id_type=MESH,
        )

    for rd in (4, 5, 3):
        w_loads[rd].wait()
    for at in range(4):
        block = ORDER[0][at][0]
        gate(block)
        for direction in range(2):
            product = jnp.dot(gated[rows_of(block), :], w_buf[relative(direction, block, 0)], preferred_element_type=F32)
            sent[direction, at] = product.astype(BF16)
            z_copy(direction, at).start()

    def products(k, _):
        rd = jnp.where(lax.rem(k, 2) == 0, 3 - lax.div(k, 2), 5 + lax.div(k, 2))
        for n in range(2):
            lanes = pl.ds(256 * n, 256)
            part[rd, :, lanes] = jnp.dot(gated[...], w_buf[rd, :, lanes], preferred_element_type=F32)
        return 0

    for rd in (2, 6):
        w_loads[rd].wait()
    lax.fori_loop(0, 4, products, 0)

    for at in range(4, UNITS):
        if at == 8:
            for rd in (1, 7, 0):
                w_loads[rd].wait()
            lax.fori_loop(4, 7, products, 0)
        for direction in range(2):
            block, step = ORDER[direction][at]
            previous = INDEX[direction][block, step - 1]
            z_copy(direction, previous).wait_recv()
            summed = part[relative(direction, block, step), rows_of(block), :] + received[direction, previous].astype(F32)
            sent[direction, at] = summed.astype(BF16)
            z_copy(direction, at).start()

    for block in (0, 2, 1, 3):
        summed = part[0, rows_of(block), :]
        for direction in range(2):
            last = INDEX[direction][block, HOPS[direction][block] - 1]
            z_copy(direction, last).wait_recv()
            summed = summed + received[direction, last].astype(F32)
        out[rows_of(block), :] = summed.astype(BF16)

    state_copies(0, lambda copy: copy.wait_send())
    state_copies(1, lambda copy: copy.wait_send())

    @pl.when(is_second)
    def _():
        for half in range(2):
            row_copies(half, lambda copy: copy.wait_send())
            core_copy(half).wait_send()

    for direction in range(2):
        for at in range(UNITS):
            z_copy(direction, at).wait_send()


def per_device(query_proj, key_projected, value_projected, mode_decay_speed, residue, out_weight):
    vmem, dma = pltpu.VMEM, pltpu.SemaphoreType.DMA
    operands = (query_proj, key_projected, value_projected, mode_decay_speed.T, residue.T, out_weight)
    return pl.pallas_call(
        kernel,
        out_shape=jax.ShapeDtypeStruct((ROWS, COLS), BF16),
        in_specs=[pl.BlockSpec(memory_space=pltpu.HBM)] * 6,
        out_specs=pl.BlockSpec(memory_space=pltpu.VMEM),
        scratch_shapes=[
            vmem((ROWS, WIDTH), BF16), vmem((ROWS, WIDTH), BF16), vmem((ROWS, WIDTH), BF16),
            vmem((16, WIDTH), F32), vmem((16, WIDTH), F32), vmem((8, WIDTH, COLS), BF16),
            vmem((128, 128), F32), vmem((128, 128), F32), vmem((128, 128), F32), vmem((128, 128), F32),
            vmem((4, 128, 128), F32), vmem((ROWS // BLOCK, 128, 128), F32), vmem((STEP * 8, 128), F32), vmem((ROWS // STEP * 128, 128), F32), vmem((ROWS * 8, 128), F32), vmem((ROWS * 8, 128), F32),
            vmem((2, 64, 128), BF16), vmem((2 * SIDE, 2, 64, 128), BF16), vmem((2, 64, 128), BF16), vmem((SIDE, 2, 64, 128), BF16),
            vmem((2 * SIDE, 128, 128), F32), vmem((2, 64, 128), F32), vmem((2, 64, 128), F32), vmem((ROWS, WIDTH), BF16), vmem((8, ROWS, COLS), F32),
            vmem((2, UNITS, BLOCK, COLS), BF16), vmem((2, UNITS, BLOCK, COLS), BF16),
            dma((5,)), dma((8,)), dma((2, SIDE)), dma((2 * SIDE, 2)), dma((SIDE, 2)), dma((SIDE, 2)), dma((2,)), dma((2,)),
            dma((2, UNITS)), dma((2, UNITS)),
        ],
        compiler_params=pltpu.CompilerParams(collective_id=0, has_side_effects=True, vmem_limit_bytes=48 << 20),
        name="hyena",
    )(*(pltpu.with_memory_space_constraint(operand, pltpu.HBM) for operand in operands))


def solution(mesh):
    return jax.shard_map(
        per_device,
        mesh=mesh,
        in_specs=(P("seq", "ch"), P("seq", "ch"), P("seq", "ch"), P("ch", None), P("ch", None), P("ch", None)),
        out_specs=P("seq", "ch"),
        check_vma=False,
    )
```

time: 41.2 us -> 39.5 us (0.959)
  Pallas kernels: 40.4 us -> 38.7 us
    pallas_call x1, Pallas kernels: 40.4 us -> 38.7 us  [per_device(): pl.pallas_call(kernel, out_shape=jax.ShapeDtypeStruct((ROWS, COLS), BF16)...]
where the time goes in v2:
time: 39.5 us; the launch traced here: 39.4 us
  Pallas kernels  38.7 us (98%)
  local copies, waits for them, and re-layouts  0.71 us (2%)
    pallas_call x1, Pallas kernels, per_device(): pl.pallas_call(kernel, out_shape=jax.ShapeDtypeStruct((ROWS, COLS), BF16)...  38.7 us

profile of v2, /device:TPU:6, one launch (start us, length us, event | category | flops | bytes accessed | tf_op | source)
XLA Modules:
  0.0 39.4 jit_solution(4423633004905217342)
XLA Ops:
  0.0 38.7 %hyena.1 = bf16[256,512]{1,0:T(8,128)(2,1)S(1)} custom-call(bf16[256,1024]{1,0:T(8,128)(2,1)} %q_hbm.1, bf16[256,1024]{1,0:T(8,128)(2,1)} %k_hbm.1, bf16[256,1024]{1,0:T(8,128)(2,1)} %v_hbm.1, f32[16,1024]{1,0:T(8,128)} %bitcast.2, f32[16,1024]{1,0:T(8,128)} %bitcast.3, bf16[1024,4096]{1,0:T(8,128)(2,1)} %w_hbm.1), custom_call_target="tpu_custom_call" | custom-call | tf_op jit(solution)/shard_map/hyena/pallas_call | solution.py:351
  38.7 0.7 %copy.8 = bf16[256,512]{1,0:T(8,128)(2,1)} copy(bf16[256,512]{1,0:T(8,128)(2,1)S(1)} %hyena.1) | data formatting | bytes 524288

commit v3 on v2

--- a/solution.py
+++ b/solution.py
@@ -18,9 +18,10 @@
 HOPS = ((4, 4, 3, 3), (3, 3, 4, 4))
 ORDER = (
     ((0, 0), (2, 0), (1, 0), (3, 0), (0, 1), (1, 1), (2, 1), (3, 1), (0, 2), (1, 2), (2, 2), (3, 2), (0, 3), (1, 3)),
-    ((0, 0), (2, 0), (1, 0), (3, 0), (2, 1), (0, 1), (3, 1), (1, 1), (2, 2), (3, 2), (0, 2), (1, 2), (2, 3), (3, 3)),
+    ((0, 0), (2, 0), (1, 0), (3, 0), (2, 1), (1, 1), (3, 1), (0, 1), (2, 2), (3, 2), (1, 2), (0, 2), (2, 3), (3, 3)),
 )
 UNITS = len(ORDER[0])
+TURNED = (5, 6, 7)
 INDEX = tuple({unit: at for at, unit in enumerate(order)} for order in ORDER)
 
 
@@ -39,13 +40,23 @@
 def kernel(
     q_hbm, k_hbm, v_hbm, decay_hbm, residue_hbm, w_hbm, out,
     q_buf, k_buf, v_buf, decay_buf, residue_buf, w_buf,
-    rate, ratio, ratio_step, weight, decays, starts, taps, kept, xs, ys, own, states, row_total, row_totals, prefixes, before, sent_before, gated, part, sent, received,
-    load_sem, w_sem, state_send, state_recv, row_send, row_recv, core_send, core_recv, z_send, z_recv,
+    rate, ratio, ratio_step, weight, decays, starts, taps, kept, xs, ys, own, states, row_total, row_totals, prefixes, before, sent_before, gated, part, sent, received, turned,
+    load_sem, w_sem, state_send, state_recv, row_ready, row_send, row_recv, core_send, core_recv, z_send, z_recv, turned_send, turned_recv,
 ):
     seq, z = lax.axis_index("seq"), lax.axis_index("ch")
     chip, core = lax.div(seq, 2), lax.rem(seq, 2)
     at_x, at_y = lax.div(chip, SIDE), lax.rem(chip, SIDE)
     is_second = core == 1
+
+    def any_of(places):
+        found = z == places[0]
+        for place in places[1:]:
+            found = found | (z == place)
+        return found
+
+    is_from = any_of(TURNED)
+    is_via = any_of([place - 1 for place in TURNED])
+    is_spared = any_of([(place + 1) % 8 for place in TURNED])
 
     def device(x, y, core_at):
         return {"seq": (x * SIDE + y) * 2 + core_at, "ch": z}
@@ -74,10 +85,15 @@
 
     @pl.when(is_second)
     def _():
+        for d in (2, 1, 3):
+            near = lax.rem(at_y + d, SIDE)
+            for partner in (device(at_x, near, 1), device(at_x, near, 0)):
+                greet(partner)
+
         for d in range(1, SIDE):
-            near = lax.rem(at_y + d, SIDE)
-            for partner in (device(lax.rem(at_x + d, SIDE), at_y, 1), device(at_x, near, 1), device(at_x, near, 0)):
-                greet(partner)
+            @pl.when(at_x + d < SIDE)
+            def _():
+                greet(device(at_x + d, at_y, 1))
 
     loads[0].wait()
     for j in range(8):
@@ -143,7 +159,11 @@
     own_state(0)
     @pl.when(is_second)
     def _():
-        pl.semaphore_wait(barrier, 3 * (SIDE - 1))
+        pl.semaphore_wait(barrier, SIDE - 1 + 3 + at_x)
+        for d in range(1, SIDE):
+            @pl.when(at_x >= d)
+            def _():
+                pl.semaphore_signal(row_ready, inc=1, device_id=device(at_x - d, at_y, 1), device_id_type=MESH)
 
     @pl.when(jnp.logical_not(is_second))
     def _():
@@ -220,6 +240,11 @@
                 prefixes[at, rows, :] = whole
                 whole = device_decay * whole + states[at, half].astype(F32)
             row_total[half] = whole.astype(BF16)
+            if half == 0:
+                @pl.when(at_x < SIDE - 1)
+                def _():
+                    pl.semaphore_wait(row_ready, SIDE - 1 - at_x)
+
             row_copies(half, lambda copy: copy.start())
 
     def core_copy(half):
@@ -289,6 +314,12 @@
             device_id=z_neighbour(direction), device_id_type=MESH,
         )
 
+    def turned_copy(block, at):
+        return pltpu.make_async_remote_copy(
+            src_ref=sent.at[0, at], dst_ref=turned.at[block], send_sem=turned_send.at[block], recv_sem=turned_recv.at[block],
+            device_id=z_neighbour(1), device_id_type=MESH,
+        )
+
     for rd in (4, 5, 3):
         w_loads[rd].wait()
     for at in range(4):
@@ -297,7 +328,34 @@
         for direction in range(2):
             product = jnp.dot(gated[rows_of(block), :], w_buf[relative(direction, block, 0)], preferred_element_type=F32)
             sent[direction, at] = product.astype(BF16)
-            z_copy(direction, at).start()
+            if block >= 1:
+                z_copy(direction, at).start()
+            elif direction == 0:
+                @pl.when(is_from)
+                def _():
+                    turned_copy(block, at).start()
+
+                @pl.when(jnp.logical_not(is_from))
+                def _():
+                    z_copy(direction, at).start()
+            else:
+                @pl.when(is_via)
+                def _():
+                    part[relative(direction, block, 0), rows_of(block), :] = product
+
+                @pl.when(jnp.logical_not(is_via))
+                def _():
+                    z_copy(direction, at).start()
+
+    def pass_on(block):
+        at = INDEX[1][block, 0]
+
+        @pl.when(is_via)
+        def _():
+            turned_copy(block, at).wait_recv()
+            summed = part[relative(1, block, 0), rows_of(block), :] + turned[block].astype(F32)
+            sent[1, at] = summed.astype(BF16)
+            z_copy(1, at).start()
 
     def products(k, _):
         rd = jnp.where(lax.rem(k, 2) == 0, 3 - lax.div(k, 2), 5 + lax.div(k, 2))
@@ -308,7 +366,9 @@
 
     for rd in (2, 6):
         w_loads[rd].wait()
-    lax.fori_loop(0, 4, products, 0)
+    lax.fori_loop(0, 2, products, 0)
+    pass_on(0)
+    lax.fori_loop(2, 4, products, 0)
 
     for at in range(4, UNITS):
         if at == 8:
@@ -318,9 +378,21 @@
         for direction in range(2):
             block, step = ORDER[direction][at]
             previous = INDEX[direction][block, step - 1]
-            z_copy(direction, previous).wait_recv()
-            summed = part[relative(direction, block, step), rows_of(block), :] + received[direction, previous].astype(F32)
-            sent[direction, at] = summed.astype(BF16)
+            spared = direction == 0 and block < 1 and step == 1
+
+            def add(direction=direction, at=at, block=block, step=step, previous=previous):
+                z_copy(direction, previous).wait_recv()
+                summed = part[relative(direction, block, step), rows_of(block), :] + received[direction, previous].astype(F32)
+                sent[direction, at] = summed.astype(BF16)
+
+            if spared:
+                pl.when(jnp.logical_not(is_spared))(add)
+
+                @pl.when(is_spared)
+                def _():
+                    sent[direction, at] = part[relative(direction, block, step), rows_of(block), :].astype(BF16)
+            else:
+                add()
             z_copy(direction, at).start()
 
     for block in (0, 2, 1, 3):
@@ -342,7 +414,17 @@
 
     for direction in range(2):
         for at in range(UNITS):
-            z_copy(direction, at).wait_send()
+            block, step = ORDER[direction][at]
+            if direction == 0 and block < 1 and step == 0:
+                @pl.when(is_from)
+                def _():
+                    turned_copy(block, at).wait_send()
+
+                @pl.when(jnp.logical_not(is_from))
+                def _():
+                    z_copy(direction, at).wait_send()
+            else:
+                z_copy(direction, at).wait_send()
 
 
 def per_device(query_proj, key_projected, value_projected, mode_decay_speed, residue, out_weight):
@@ -360,9 +442,9 @@
             vmem((4, 128, 128), F32), vmem((ROWS // BLOCK, 128, 128), F32), vmem((STEP * 8, 128), F32), vmem((ROWS // STEP * 128, 128), F32), vmem((ROWS * 8, 128), F32), vmem((ROWS * 8, 128), F32),
             vmem((2, 64, 128), BF16), vmem((2 * SIDE, 2, 64, 128), BF16), vmem((2, 64, 128), BF16), vmem((SIDE, 2, 64, 128), BF16),
             vmem((2 * SIDE, 128, 128), F32), vmem((2, 64, 128), F32), vmem((2, 64, 128), F32), vmem((ROWS, WIDTH), BF16), vmem((8, ROWS, COLS), F32),
-            vmem((2, UNITS, BLOCK, COLS), BF16), vmem((2, UNITS, BLOCK, COLS), BF16),
-            dma((5,)), dma((8,)), dma((2, SIDE)), dma((2 * SIDE, 2)), dma((SIDE, 2)), dma((SIDE, 2)), dma((2,)), dma((2,)),
-            dma((2, UNITS)), dma((2, UNITS)),
+            vmem((2, UNITS, BLOCK, COLS), BF16), vmem((2, UNITS, BLOCK, COLS), BF16), vmem((1, BLOCK, COLS), BF16),
+            dma((5,)), dma((8,)), dma((2, SIDE)), dma((2 * SIDE, 2)), pltpu.SemaphoreType.REGULAR, dma((SIDE, 2)), dma((SIDE, 2)), dma((2,)), dma((2,)),
+            dma((2, UNITS)), dma((2, UNITS)), dma((1,)), dma((1,)),
         ],
         compiler_params=pltpu.CompilerParams(collective_id=0, has_side_effects=True, vmem_limit_bytes=48 << 20),
         name="hyena",

time: 39.5 us -> 39.2 us (level)
  no operation moved by 1% of the time
where the time goes in v3:
time: 39.2 us; the launch traced here: 39.1 us
  Pallas kernels  38.4 us (98%)
  local copies, waits for them, and re-layouts  0.71 us (2%)
    pallas_call x1, Pallas kernels, per_device(): pl.pallas_call(kernel, out_shape=jax.ShapeDtypeStruct((ROWS, COLS), BF16)...  38.4 us

profile of v3, /device:TPU:6, one launch (start us, length us, event | category | flops | bytes accessed | tf_op | source)
XLA Modules:
  0.0 39.1 jit_solution(11278297517141553425)
XLA Ops:
  0.0 38.4 %hyena.1 = bf16[256,512]{1,0:T(8,128)(2,1)S(1)} custom-call(bf16[256,1024]{1,0:T(8,128)(2,1)} %q_hbm.1, bf16[256,1024]{1,0:T(8,128)(2,1)} %k_hbm.1, bf16[256,1024]{1,0:T(8,128)(2,1)} %v_hbm.1, f32[16,1024]{1,0:T(8,128)} %bitcast.2, f32[16,1024]{1,0:T(8,128)} %bitcast.3, bf16[1024,4096]{1,0:T(8,128)(2,1)} %w_hbm.1), custom_call_target="tpu_custom_call" | custom-call | tf_op jit(solution)/shard_map/hyena/pallas_call | solution.py:433
  38.4 0.7 %copy.8 = bf16[256,512]{1,0:T(8,128)(2,1)} copy(bf16[256,512]{1,0:T(8,128)(2,1)S(1)} %hyena.1) | data formatting | bytes 524288

commit v4 on v3

--- a/solution.py
+++ b/solution.py
@@ -322,30 +322,41 @@
 
     for rd in (4, 5, 3):
         w_loads[rd].wait()
-    for at in range(4):
+    def leave(direction, at):
         block = ORDER[0][at][0]
-        gate(block)
-        for direction in range(2):
-            product = jnp.dot(gated[rows_of(block), :], w_buf[relative(direction, block, 0)], preferred_element_type=F32)
-            sent[direction, at] = product.astype(BF16)
-            if block >= 1:
+        product = jnp.dot(gated[rows_of(block), :], w_buf[relative(direction, block, 0)], preferred_element_type=F32)
+        sent[direction, at] = product.astype(BF16)
+        if block >= 1:
+            z_copy(direction, at).start()
+        elif direction == 0:
+            @pl.when(is_from)
+            def _():
+                turned_copy(block, at).start()
+
+            @pl.when(jnp.logical_not(is_from))
+            def _():
                 z_copy(direction, at).start()
-            elif direction == 0:
-                @pl.when(is_from)
-                def _():
-                    turned_copy(block, at).start()
-
-                @pl.when(jnp.logical_not(is_from))
-                def _():
-                    z_copy(direction, at).start()
-            else:
-                @pl.when(is_via)
-                def _():
-                    part[relative(direction, block, 0), rows_of(block), :] = product
-
-                @pl.when(jnp.logical_not(is_via))
-                def _():
-                    z_copy(direction, at).start()
+        else:
+            @pl.when(is_via)
+            def _():
+                part[relative(direction, block, 0), rows_of(block), :] = product
+
+            @pl.when(jnp.logical_not(is_via))
+            def _():
+                z_copy(direction, at).start()
+
+    gate(ORDER[0][0][0])
+    leave(0, 0)
+    gate(ORDER[0][1][0])
+    leave(0, 1)
+    leave(1, 0)
+    gate(ORDER[0][2][0])
+    leave(0, 2)
+    leave(1, 1)
+    gate(ORDER[0][3][0])
+    leave(0, 3)
+    leave(1, 2)
+    leave(1, 3)
 
     def pass_on(block):
         at = INDEX[1][block, 0]

time: 39.2 us -> 38.9 us (level)
  no operation moved by 1% of the time
where the time goes in v4:
time: 38.9 us; the launch traced here: 38.8 us
  Pallas kernels  38.1 us (98%)
  local copies, waits for them, and re-layouts  0.71 us (2%)
    pallas_call x1, Pallas kernels, per_device(): pl.pallas_call(kernel, out_shape=jax.ShapeDtypeStruct((ROWS, COLS), BF16)...  38.1 us

profile of v4, /device:TPU:6, one launch (start us, length us, event | category | flops | bytes accessed | tf_op | source)
XLA Modules:
  0.0 38.8 jit_solution(15230499970775126202)
XLA Ops:
  0.0 38.1 %hyena.1 = bf16[256,512]{1,0:T(8,128)(2,1)S(1)} custom-call(bf16[256,1024]{1,0:T(8,128)(2,1)} %q_hbm.1, bf16[256,1024]{1,0:T(8,128)(2,1)} %k_hbm.1, bf16[256,1024]{1,0:T(8,128)(2,1)} %v_hbm.1, f32[16,1024]{1,0:T(8,128)} %bitcast.2, f32[16,1024]{1,0:T(8,128)} %bitcast.3, bf16[1024,4096]{1,0:T(8,128)(2,1)} %w_hbm.1), custom_call_target="tpu_custom_call" | custom-call | tf_op jit(solution)/shard_map/hyena/pallas_call | solution.py:444
  38.1 0.7 %copy.8 = bf16[256,512]{1,0:T(8,128)(2,1)} copy(bf16[256,512]{1,0:T(8,128)(2,1)S(1)} %hyena.1) | data formatting | bytes 524288

commit v5 on v4

--- a/solution.py
+++ b/solution.py
@@ -40,7 +40,7 @@
 def kernel(
     q_hbm, k_hbm, v_hbm, decay_hbm, residue_hbm, w_hbm, out,
     q_buf, k_buf, v_buf, decay_buf, residue_buf, w_buf,
-    rate, ratio, ratio_step, weight, decays, starts, taps, kept, xs, ys, own, states, row_total, row_totals, prefixes, before, sent_before, gated, part, sent, received, turned,
+    staged, rate, ratio, ratio_step, weight, decays, starts, taps, kept, xs, ys, own, states, row_total, row_totals, prefixes, before, sent_before, gated, part, sent, received, turned,
     load_sem, w_sem, state_send, state_recv, row_ready, row_send, row_recv, core_send, core_recv, z_send, z_recv, turned_send, turned_recv,
 ):
     seq, z = lax.axis_index("seq"), lax.axis_index("ch")
@@ -97,7 +97,8 @@
 
     loads[0].wait()
     for j in range(8):
-        rate[pl.ds(j, 16, stride=8), :] = decay_buf[:, pl.ds(128 * j, 128)]
+        staged[pl.ds(j, 16, stride=8), :] = decay_buf[:, pl.ds(128 * j, 128)]
+    rate[...] = staged[pl.ds(0, 128), :]
     ratio[...] = jnp.exp(-rate[...])
     ratio_step[...] = jnp.exp(-float(STEP) * rate[...])
 
@@ -185,8 +186,8 @@
 
     loads[3].wait()
     for j in range(8):
-        weight[pl.ds(j, 16, stride=8), :] = residue_buf[:, pl.ds(128 * j, 128)]
-    weight[...] = weight[...] * jnp.sqrt(one_minus_exp(2.0 * rate[...]))
+        staged[pl.ds(j, 16, stride=8), :] = residue_buf[:, pl.ds(128 * j, 128)]
+    weight[...] = staged[pl.ds(0, 128), :] * jnp.sqrt(one_minus_exp(2.0 * rate[...]))
     decays[0] = jnp.exp(-float(ROWS) * rate[...])
     decays[1] = jnp.exp(-float(2 * SIDE * ROWS) * rate[...])
     for core_at in range(2):
@@ -449,8 +450,9 @@
         scratch_shapes=[
             vmem((ROWS, WIDTH), BF16), vmem((ROWS, WIDTH), BF16), vmem((ROWS, WIDTH), BF16),
             vmem((16, WIDTH), F32), vmem((16, WIDTH), F32), vmem((8, WIDTH, COLS), BF16),
+            vmem((136, 128), F32),
             vmem((128, 128), F32), vmem((128, 128), F32), vmem((128, 128), F32), vmem((128, 128), F32),
-            vmem((4, 128, 128), F32), vmem((ROWS // BLOCK, 128, 128), F32), vmem((STEP * 8, 128), F32), vmem((ROWS // STEP * 128, 128), F32), vmem((ROWS * 8, 128), F32), vmem((ROWS * 8, 128), F32),
+            vmem((4, 128, 128), F32), vmem((ROWS // BLOCK, 128, 128), F32), vmem((STEP * 8, 128), F32), vmem((ROWS // STEP * 128, 128), F32), vmem((ROWS * 8 + 8, 128), F32), vmem((ROWS * 8 + 8, 128), F32),
             vmem((2, 64, 128), BF16), vmem((2 * SIDE, 2, 64, 128), BF16), vmem((2, 64, 128), BF16), vmem((SIDE, 2, 64, 128), BF16),
             vmem((2 * SIDE, 128, 128), F32), vmem((2, 64, 128), F32), vmem((2, 64, 128), F32), vmem((ROWS, WIDTH), BF16), vmem((8, ROWS, COLS), F32),
             vmem((2, UNITS, BLOCK, COLS), BF16), vmem((2, UNITS, BLOCK, COLS), BF16), vmem((1, BLOCK, COLS), BF16),

time: 38.9 us -> 39 us (level)
  no operation moved by 1% of the time
where the time goes in v5:
time: 39 us; the launch traced here: 38.8 us
  Pallas kernels  38.1 us (98%)
  local copies, waits for them, and re-layouts  0.71 us (2%)
    pallas_call x1, Pallas kernels, per_device(): pl.pallas_call(kernel, out_shape=jax.ShapeDtypeStruct((ROWS, COLS), BF16)...  38.1 us

profile of v5, /device:TPU:6, one launch (start us, length us, event | category | flops | bytes accessed | tf_op | source)
XLA Modules:
  0.0 38.8 jit_solution(12601949777479344947)
XLA Ops:
  0.0 38.1 %hyena.1 = bf16[256,512]{1,0:T(8,128)(2,1)S(1)} custom-call(bf16[256,1024]{1,0:T(8,128)(2,1)} %q_hbm.1, bf16[256,1024]{1,0:T(8,128)(2,1)} %k_hbm.1, bf16[256,1024]{1,0:T(8,128)(2,1)} %v_hbm.1, f32[16,1024]{1,0:T(8,128)} %bitcast.2, f32[16,1024]{1,0:T(8,128)} %bitcast.3, bf16[1024,4096]{1,0:T(8,128)(2,1)} %w_hbm.1), custom_call_target="tpu_custom_call" | custom-call | tf_op jit(solution)/shard_map/hyena/pallas_call | solution.py:445
  38.1 0.7 %copy.8 = bf16[256,512]{1,0:T(8,128)(2,1)} copy(bf16[256,512]{1,0:T(8,128)(2,1)S(1)} %hyena.1) | data formatting | bytes 524288
